TPU v7x, 512 devices: a whole 4x4x16 slice. The times are simulated.
512 devices in a mesh: region: 128 (over x, z, core), slab: 4 (over y).
Axes of the slice: x: 4, y: 4, z: 16, core: 2. Of those that a mesh axis runs over, the one named last changes fastest.
Arguments:
- features: bfloat16 [13312, 4, 4, 4, 128], P(('region', 'slab')), may hold values from -6 to 6
- weight: bfloat16 [27, 128, 128], replicated, may hold values from -0.109375 to 0.109375
- cotangent: bfloat16 [13312, 4, 4, 4, 128], P(('region', 'slab')), may hold values from -6 to 6
- occupancy: int32 [13312, 64], P(('region', 'slab')), may hold values 0 or 1
- neighbors: int32 [13312, 6], P(('region', 'slab')), may hold values from -1 to 13311, as said below
Outputs:
- output: bfloat16 [13312, 4, 4, 4, 128], P(('region', 'slab'))
- input_grad: bfloat16 [13312, 4, 4, 4, 128], P(('region', 'slab'))
- weight_grad: float32 [27, 128, 128], replicated
Inputs may be any that keep to these rules, and one draw needn't show every extreme that they name: `neighbors`: links are mutual: if the +d entry of brick a is b, the -d entry of b is a. A third-dimension entry names the brick with the same position in its device's block on the device one slab index lower or higher. Every first- and second-dimension entry names a brick of a device with the same slab index and a region index that differs by a step of 1 to 64 modulo 128; for a given slab index, dimension and sender's brick position that step is the same on every region index. One device sends at most 2 first- and second-dimension faces to any other device, and that many is reached.
All inputs are finite; a program needn't handle non-finite values. No bound on the sum of `occupancy` on one device may be relied on, other than what follows from the above.
Results may differ from a plain program's by a relative error of at most 0.0029.
Values may be sent and summed in bfloat16 or wider, within the bound.
A program may use at most 64 MiB of HBM per device.

v0:
```python
import jax
import jax.numpy as jnp
from jax import lax
from jax.sharding import PartitionSpec as P


def with_halo(block, sides, width):
    for axis, dim in sides:
        count = lax.axis_size(axis)
        forward = [(i, i + 1) for i in range(count - 1)]
        backward = [(target, source) for source, target in forward]
        low = lax.ppermute(
            lax.slice_in_dim(block, block.shape[dim] - width, None, axis=dim), axis, forward
        )
        high = lax.ppermute(lax.slice_in_dim(block, 0, width, axis=dim), axis, backward)
        block = jnp.concatenate([low, block, high], axis=dim)
    return block


def assemble_brick(stacked, planes):
    z_rim = ((0, 0), (0, 0), (1, 1), (0, 0))
    xy_rim = ((0, 0), (1, 1), (1, 1), (0, 0))
    lower_y = jnp.pad(planes[:, 2], z_rim)[:, :, None]
    upper_y = jnp.pad(planes[:, 3], z_rim)[:, :, None]
    middle = jnp.concatenate([lower_y, stacked, upper_y], axis=2)
    lower_x = jnp.pad(planes[:, 0], xy_rim)[:, None]
    upper_x = jnp.pad(planes[:, 1], xy_rim)[:, None]
    return jnp.concatenate([lower_x, middle, upper_x], axis=1)


def convolve(padded, kernel):
    bricks_here = padded.shape[0]
    channels = padded.shape[-1]
    edge = padded.shape[1] - 2
    accumulated = jnp.zeros((bricks_here * edge**3, kernel.shape[-1]), jnp.float32)
    for tap_index in range(27):
        first_offset, second_offset, third_offset = (
            tap_index // 9,
            tap_index // 3 % 3,
            tap_index % 3,
        )
        window = padded[
            :,
            first_offset : first_offset + edge,
            second_offset : second_offset + edge,
            third_offset : third_offset + edge,
        ].reshape(-1, channels)
        accumulated = accumulated + jnp.dot(
            window, kernel[tap_index], preferred_element_type=jnp.float32
        )
    return accumulated.reshape(bricks_here, edge, edge, edge, -1)


def conv_with(stacked, planes, kernel):
    result = convolve(assemble_brick(stacked, planes), kernel)
    return result


def shards(features, weight, cotangent, occupancy, neighbors):
    bricks_here = features.shape[0]
    edge = features.shape[1]
    channels = features.shape[-1]
    regions = lax.axis_size("region")
    slabs = lax.axis_size("slab")
    half_steps = regions // 2
    capacity = max(2 - regions % 2, (2 * bricks_here - 2 + half_steps - 3) // (half_steps - 2))
    item_count = 4 * bricks_here
    linked = neighbors[:, :4].reshape(item_count)
    present = linked >= 0
    owner = jnp.where(present, linked // (bricks_here * slabs), -1)
    position = linked % bricks_here
    ordinal = jnp.arange(item_count, dtype=jnp.int32)
    same_owner = owner[:, None] == owner[None, :]
    send_rank = jnp.sum(same_owner & (ordinal[None, :] < ordinal[:, None]), axis=1)
    send_slot = jnp.where(present, owner * capacity + send_rank, -1)
    side_number = ordinal % 4
    wanted_key = position * 4 + side_number + 1 - 2 * (side_number % 2)
    receive_rank = jnp.sum(same_owner & (wanted_key[None, :] < wanted_key[:, None]), axis=1)
    receive_slot = jnp.where(present, owner * capacity + receive_rank, -1)
    slot_ids = jnp.arange(regions * capacity, dtype=jnp.int32)
    packing = (slot_ids[:, None] == send_slot[None, :]).astype(jnp.bfloat16)
    unpacking = (receive_slot[:, None] == slot_ids[None, :]).astype(jnp.bfloat16)
    lower_keep = (neighbors[:, 4] >= 0).astype(jnp.bfloat16)
    upper_keep = (neighbors[:, 5] >= 0).astype(jnp.bfloat16)
    third_mask = jnp.concatenate(
        [lower_keep[:, None], jnp.ones((bricks_here, edge), jnp.bfloat16), upper_keep[:, None]],
        axis=1,
    )[:, None, None, :, None]

    def brick_pads(source):
        stacked = with_halo(source, (("slab", 3),), 1) * third_mask
        faces = jnp.stack(
            [source[:, 0], source[:, -1], source[:, :, 0], source[:, :, -1]], axis=1
        ).reshape(item_count, edge * edge * channels)
        outgoing = (
            jnp.dot(packing, faces, preferred_element_type=jnp.float32)
            .astype(jnp.bfloat16)
            .reshape(regions, capacity, edge * edge * channels)
        )
        incoming = lax.all_to_all(
            outgoing, "region", split_axis=0, concat_axis=0, tiled=True
        ).reshape(regions * capacity, edge * edge * channels)
        planes = (
            jnp.dot(unpacking, incoming, preferred_element_type=jnp.float32)
            .astype(jnp.bfloat16)
            .reshape(bricks_here, 4, edge, edge, channels)
        )
        return (stacked, planes)

    occupied = occupancy.astype(jnp.float32).reshape(bricks_here, edge, edge, edge, 1)
    flipped = jnp.swapaxes(weight[::-1], 1, 2)
    feature_stack, feature_planes = brick_pads(features)
    pre = conv_with(feature_stack, feature_planes, weight)
    sigma = jax.nn.sigmoid(pre)
    output = (features.astype(jnp.float32) + occupied * pre * sigma).astype(jnp.bfloat16)
    pre_grad = (
        cotangent.astype(jnp.float32) * occupied * sigma * (1.0 + pre * (1.0 - sigma))
    ).astype(jnp.bfloat16)
    grad_stack, grad_planes = brick_pads(pre_grad)
    back = conv_with(grad_stack, grad_planes, flipped)
    input_grad = (cotangent.astype(jnp.float32) + back).astype(jnp.bfloat16)
    padded = assemble_brick(feature_stack, feature_planes)
    flat_grad = pre_grad.reshape(-1, channels)
    pieces = []
    for tap_index in range(27):
        first_offset, second_offset, third_offset = (
            tap_index // 9,
            tap_index // 3 % 3,
            tap_index % 3,
        )
        window = padded[
            :,
            first_offset : first_offset + edge,
            second_offset : second_offset + edge,
            third_offset : third_offset + edge,
        ].reshape(-1, channels)
        pieces.append(
            jnp.einsum("rc,rd->cd", window, flat_grad, preferred_element_type=jnp.float32)
        )
    local_grad = jnp.stack(pieces, axis=0)
    summed = lax.psum(local_grad, ("region", "slab"))
    weight_grad = summed * (bricks_here * regions * slabs * float(edge**3)) ** (-0.5)
    return (output, input_grad, weight_grad)


def solution(mesh):
    return jax.shard_map(
        shards,
        mesh=mesh,
        in_specs=(
            P(("region", "slab"), None, None, None, None),
            P(),
            P(("region", "slab"), None, None, None, None),
            P(("region", "slab"), None),
            P(("region", "slab"), None),
        ),
        out_specs=(
            P(("region", "slab"), None, None, None, None),
            P(("region", "slab"), None, None, None, None),
            P(),
        ),
        check_vma=False,
    )
```

profile of v0, /device:TPU:25, one launch (start us, length us, event | category | flops | bytes accessed | tf_op | source)
XLA Modules:
  0.0 654.4 jit_solution(17086320830689203417)
XLA Ops:
  7.2 1.0 slice_bitcast_fusion.3
  8.2 1.0 slice_bitcast_fusion.5
  13.1 1.5 reshape.389
  14.6 19.7 %all-to-all-start = ((bf16[128,2,2048]{2,1,0:T(2,128)(2,1)}), bf16[128,2,2048]{2,1,0:T(2,128)(2,1)S(1)}, u32[]{:S(2)}, u32[]{:S(2)}) async-start(bf16[128,2,2048]{2,1,0:T(2,128)(2,1)} %reshape.389), calls=%async_computation | async-start | bytes 2097152 | tf_op jit(solution)/shard_map/all_to_all | solution.py:100
  34.6 2.4 collective-permute-start.1
  37.0 1.3 collective-permute-start
  39.3 3.7 collective-permute-done
  43.2 45.5 %all-to-all-done = bf16[128,2,2048]{2,1,0:T(2,128)(2,1)S(1)} async-done(((bf16[128,2,2048]{2,1,0:T(2,128)(2,1)}), bf16[128,2,2048]{2,1,0:T(2,128)(2,1)S(1)}, u32[]{:S(2)}, u32[]{:S(2)}) %all-to-all-start) | async-done | bytes 1048608 | tf_op jit(solution)/shard_map/all_to_all | solution.py:100
  107.5 2.7 fusion.35
  110.3 1.0 fusion.26
  112.3 1.5 reshape.421
  113.8 8.5 %all-to-all-start.1 = ((bf16[128,2,2048]{2,1,0:T(2,128)(2,1)}), bf16[128,2,2048]{2,1,0:T(2,128)(2,1)S(1)}, u32[]{:S(2)}, u32[]{:S(2)}) async-start(bf16[128,2,2048]{2,1,0:T(2,128)(2,1)} %reshape.421), calls=%async_computation.1 | async-start | bytes 2097152 | tf_op jit(solution)/shard_map/all_to_all | solution.py:100
  122.4 1.9 fusion.25
  124.3 1.0 fusion.24
  125.3 1.0 fusion.23
  126.3 1.0 fusion.22
  127.3 1.0 fusion.21
  128.2 1.0 fusion.20
  129.2 1.0 fusion.19
  130.2 1.0 fusion.18
  141.9 1.0 fusion.12
  144.8 1.0 fusion.9
  145.8 1.0 fusion.8
  147.7 1.0 fusion.6
  148.7 2.5 collective-permute-start.3
  151.3 1.3 collective-permute-start.2
  152.6 1.0 reverse_bitcast_fusion
  153.6 1.0 copy.202
  154.5 2.7 collective-permute-done.2
  157.4 466.3 %all-reduce.10.cloned.1.call-done = f32[27,128,128]{2,1,0:T(8,128)} async-done(((f32[27,128,128]{2,1,0:T(8,128)}), f32[27,128,128]{2,1,0:T(8,128)}) %all-reduce.10.cloned.1.call-update) | async-done | bytes 1769488 | tf_op jit(solution)/shard_map/psum | solution.py:141
  623.8 2.9 broadcast_multiply_fusion
  646.2 1.0 copy.203
  (220 shorter events, 57.5 us)
Async XLA Ops:
  13.1 21.2 %copy-start = (bf16[26,4,4,4,128]{4,3,2,1,0:T(4,128)(2,1)S(1)}, bf16[26,4,4,4,128]{4,3,2,1,0:T(4,128)(2,1)}, u32[]{:S(2)}) copy-start(bf16[26,4,4,4,128]{4,3,2,1,0:T(4,128)(2,1)} %param.5) | copy-start | bytes 1277956
  14.6 24.7 %copy-start.12 = (s32[26,64]{1,0:T(8,128)S(1)}, s32[26,64]{1,0:T(8,128)}, u32[]{:S(2)}) copy-start(s32[26,64]{1,0:T(8,128)} %param.8) | copy-start | bytes 19972
  14.6 74.1 %all-to-all-start = ((bf16[128,2,2048]{2,1,0:T(2,128)(2,1)}), bf16[128,2,2048]{2,1,0:T(2,128)(2,1)S(1)}, u32[]{:S(2)}, u32[]{:S(2)}) async-start(bf16[128,2,2048]{2,1,0:T(2,128)(2,1)} %reshape.389), calls=%async_computation | async-start | bytes 2097152 | tf_op jit(solution)/shard_map/all_to_all | solution.py:100
  34.6 4.7 collective-permute-start.1
  37.0 6.0 collective-permute-start
  89.9 0.8 copy-start.8
  90.1 20.2 %copy-start.5 = (bf16[26,4,1,6,128]{4,0,3,2,1:T(8,128)(2,1)}, bf16[26,4,1,6,128]{4,0,3,2,1:T(8,128)(2,1)S(1)}, u32[]{:S(2)}) copy-start(bf16[26,4,1,6,128]{4,0,3,2,1:T(8,128)(2,1)S(1)} %pad_bitcast_fusion.7) | copy-start | bytes 479236
  90.2 20.1 %copy-start.10 = (bf16[26,1,6,6,128]{4,0,3,2,1:T(8,128)(2,1)}, bf16[26,1,6,6,128]{4,0,3,2,1:T(8,128)(2,1)S(1)}, u32[]{:S(2)}) copy-start(bf16[26,1,6,6,128]{4,0,3,2,1:T(8,128)(2,1)S(1)} %pad_bitcast_fusion.3) | copy-start | bytes 718852
  98.8 1.2 copy-start.1
  106.5 1.0 copy-start.7
  112.3 10.0 %copy-start.6 = (bf16[26,4,1,6,128]{4,0,3,2,1:T(8,128)(2,1)S(1)}, bf16[26,4,1,6,128]{4,0,3,2,1:T(8,128)(2,1)}, u32[]{:S(2)}) copy-start(bf16[26,4,1,6,128]{4,0,3,2,1:T(8,128)(2,1)} %copy-done.5) | copy-start | bytes 479236
  113.8 512.9 %all-to-all-start.1 = ((bf16[128,2,2048]{2,1,0:T(2,128)(2,1)}), bf16[128,2,2048]{2,1,0:T(2,128)(2,1)S(1)}, u32[]{:S(2)}, u32[]{:S(2)}) async-start(bf16[128,2,2048]{2,1,0:T(2,128)(2,1)} %reshape.421), calls=%async_computation.1 | async-start | bytes 2097152 | tf_op jit(solution)/shard_map/all_to_all | solution.py:100
  122.3 501.5 %all-reduce.10.cloned.1.call-start = ((), (), s32[]{:S(2)}) async-start(), calls=%async_computation.2 | async-start | bytes 3538944 | tf_op jit(solution)/shard_map/psum | solution.py:141
  122.4 2.0 copy-start.11
  138.9 1.0 copy-start.9
  148.7 3.9 copy-start.2
  148.7 4.9 copy-start.4
  148.7 5.8 collective-permute-start.3
  151.3 6.0 collective-permute-start.2
  636.6 1.2 copy-start.3
Sparse Core Ops, SparseCore 0:
  148.8 474.8 all-reduce.9
where the time goes:
time: 661 us; the launch traced here: 654 us
  waiting for transfers between devices  518 us (78%)
  matrix products  43 us (7%)
  starting transfers between devices  35.7 us (5%)
  local copies, waits for them, and re-layouts  29.3 us (4%)
  between operations  15.7 us (2%)
  other arithmetic  12.5 us (2%)
    psum x1, waiting for transfers between devices, shards(): summed = lax.psum(local_grad, ('region', 'slab'))  466 us
    all_to_all x2, waiting for transfers between devices, brick_pads(): lax.all_to_all(outgoing, 'region', split_axis=0, concat_axis=0, tiled=True)  45.5 us
    all_to_all x2, starting transfers between devices, brick_pads(): lax.all_to_all(outgoing, 'region', split_axis=0, concat_axis=0, tiled=True)  28.2 us
    dot_general x27, matrix products, shards(): jnp.einsum('rc,rd->cd', window, flat_grad, preferred_element_type=jnp.flo...  27.3 us
    slice x58, local copies, waits for them, and re-layouts, convolve(): padded[:, first_offset:first_offset + edge, second_offset:second_offset +...  15.6 us
    dot_general x54, matrix products, convolve(): jnp.dot(window, kernel[tap_index], preferred_element_type=jnp.float32)  14.2 us
  transfers between devices with their start and end apart: 7, of which 4 were waited for; matrix products, arithmetic and copies ran while one was open for 5% of the time, Pallas kernels for 0%

commit v1 on v0

v1 whole, which is shorter than its diff:
```python
import functools

import jax
import jax.numpy as jnp
from jax import lax
from jax.experimental import pallas as pl
from jax.experimental.pallas import tpu as pltpu
from jax.sharding import PartitionSpec as P

MESH = pl.DeviceIdType.MESH
BF = jnp.bfloat16
F32 = jnp.float32

CH = 128
BD = 26
BP = 32
VOX = 64
REG = 128
SLB = 4
NX, NZ, NCORE = 4, 16, 2
NXY = NX * SLB
SLOTS = 2 * REG
TAPS = 27
TPAD = 32
HALF_T = TPAD // 2
VMEM_LIMIT = 50 * 1024 * 1024


def params(**kw):
    return pltpu.CompilerParams(vmem_limit_bytes=VMEM_LIMIT, **kw)


def vmem(shape, dtype):
    return jax.ShapeDtypeStruct(shape, dtype)


IN_VMEM = pl.BlockSpec(memory_space=pltpu.VMEM)
IN_SMEM = pl.BlockSpec(memory_space=pltpu.SMEM)
IN_ANY = pl.BlockSpec(memory_space=pl.ANY)


def face_voxels(side):
    if side == 0:
        return [4 * a + b for a in range(4) for b in range(4)]
    if side == 1:
        return [48 + 4 * a + b for a in range(4) for b in range(4)]
    if side == 2:
        return [16 * a + b for a in range(4) for b in range(4)]
    return [16 * a + 12 + b for a in range(4) for b in range(4)]


def fill_faces(slabs, faces):
    for side in range(4):
        for t, v in enumerate(face_voxels(side)):
            faces[side, pl.ds(t, BP, stride=16), :] = slabs(v)


def pack_slots(faces, slot_ref, slots):
    for side in range(4):

        def body(b, carry):
            slot = slot_ref[side * BD + b]
            tile = faces[side, pl.ds(pl.multiple_of(b * 16, 16), 16), :]
            slots[pl.ds(pl.multiple_of(slot * 16, 16), 16), :] = tile.astype(BF)
            return carry

        lax.fori_loop(0, BD, body, 0)


def pack_kernel(feat, slot_ref, x_ref, slots, rows, faces):
    rows[0 : BD * VOX, :] = feat[...].astype(F32)
    rows[BD * VOX :, :] = jnp.zeros((BP * VOX - BD * VOX, CH), F32)
    for v in range(VOX):
        x_ref[v] = rows[pl.ds(v, BP, stride=VOX), :].astype(BF)
    fill_faces(lambda v: rows[pl.ds(v, BP, stride=VOX), :], faces)
    pack_slots(faces, slot_ref, slots)


def exchange_start(me, slab, slots, recv, x_ref, low, high, sems):
    send_sem, recv_sem, z_send, z_recv = sems
    up = lax.rem(slab + 1, SLB)
    down = lax.rem(slab + SLB - 1, SLB)
    to_up = pltpu.make_async_remote_copy(
        x_ref.at[:, 3], low, z_send.at[0], z_recv.at[0],
        device_id={"region": me, "slab": up}, device_id_type=MESH)
    to_down = pltpu.make_async_remote_copy(
        x_ref.at[:, 0], high, z_send.at[1], z_recv.at[1],
        device_id={"region": me, "slab": down}, device_id_type=MESH)

    def send(k, carry):
        peer = lax.rem(me + k, REG)
        pltpu.make_async_remote_copy(
            slots.at[pl.ds(pl.multiple_of(peer * 32, 32), 32)],
            recv.at[pl.ds(pl.multiple_of(me * 32, 32), 32)],
            send_sem, recv_sem,
            device_id={"region": peer, "slab": slab}, device_id_type=MESH,
        ).start()
        return carry

    lax.fori_loop(1, REG, send, 0)
    to_up.start()
    to_down.start()
    return to_up, to_down


def exchange_wait(slots, recv, sems, pair):
    send_sem, recv_sem, _, _ = sems
    span = pl.ds(0, (REG - 1) * 32)
    pltpu.make_async_copy(recv.at[span], recv.at[span], recv_sem).wait()
    pltpu.make_async_copy(slots.at[span], slots.at[span], send_sem).wait()
    for copy in pair:
        copy.wait()


def region_barrier(me, slab, barrier):
    def greet(k, carry):
        pl.semaphore_signal(
            barrier, inc=1, device_id={"region": lax.rem(me + k, REG), "slab": slab},
            device_id_type=MESH)
        return carry

    lax.fori_loop(1, REG, greet, 0)


def first_exchange(slots, x_ref, recv, low, high, send_sem, recv_sem, z_send, z_recv):
    me = lax.axis_index("region")
    slab = lax.axis_index("slab")
    barrier = pltpu.get_barrier_semaphore()
    region_barrier(me, slab, barrier)
    for step in (1, SLB - 1):
        pl.semaphore_signal(
            barrier, inc=1, device_id={"region": me, "slab": lax.rem(slab + step, SLB)},
            device_id_type=MESH)
    pl.semaphore_wait(barrier, REG - 1 + 2)
    sems = (send_sem, recv_sem, z_send, z_recv)
    pair = exchange_start(me, slab, slots, recv, x_ref, low, high, sems)
    exchange_wait(slots, recv, sems, pair)


def second_exchange(slots, x_ref, grad, recv, low, high, total, part, col, mine, got0, got1, got2,
                    send_sem, recv_sem, z_send, z_recv, a_sem, b_sem, c_sem, d_sem, e_sem, f_sem):
    me = lax.axis_index("region")
    slab = lax.axis_index("slab")
    x = me // (NZ * NCORE)
    z = lax.rem(me // NCORE, NZ)
    core = lax.rem(me, NCORE)
    q = x * SLB + slab

    def region_of(xx, zz, cc):
        return (xx * NZ + zz) * NCORE + cc

    def xy_peer(k):
        other = lax.rem(q + k, NXY)
        return other, {"region": region_of(other // SLB, z, core), "slab": lax.rem(other, SLB)}

    def z_peer(k):
        other = lax.rem(z + k, NZ)
        return other, {"region": region_of(x, other, core), "slab": slab}

    partner = {"region": region_of(x, z, 1 - core), "slab": slab}

    barrier = pltpu.get_barrier_semaphore()
    region_barrier(me, slab, barrier)

    def greet(k, carry):
        s = lax.rem(slab + 1 + lax.rem(k, SLB - 1), SLB)
        pl.semaphore_signal(
            barrier, inc=1, device_id={"region": region_of(k // (SLB - 1), z, core), "slab": s},
            device_id_type=MESH)
        return carry

    lax.fori_loop(0, NX * (SLB - 1), greet, 0)
    pl.semaphore_wait(barrier, REG - 1 + NX * (SLB - 1))

    own = pl.ds(pl.multiple_of(core * HALF_T, HALF_T), HALF_T)
    other_half = pl.ds(pl.multiple_of((1 - core) * HALF_T, HALF_T), HALF_T)
    pair0 = pltpu.make_async_remote_copy(
        grad.at[other_half], got0, a_sem.at[0], a_sem.at[1], device_id=partner, device_id_type=MESH)
    pair0.start()
    sems = (send_sem, recv_sem, z_send, z_recv)
    zpair = exchange_start(me, slab, slots, recv, x_ref, low, high, sems)
    pair0.wait()

    def add_pair(t, carry):
        part[t] = grad[core * HALF_T + t] + got0[t]
        return carry

    lax.fori_loop(0, HALF_T, add_pair, 0)

    def send1(k, carry):
        other, device = xy_peer(k)
        pltpu.make_async_remote_copy(
            part.at[:, pl.ds(pl.multiple_of(other * 8, 8), 8)], got1.at[q],
            b_sem.at[0], b_sem.at[1], device_id=device, device_id_type=MESH).start()
        return carry

    lax.fori_loop(1, NXY, send1, 0)
    got1[q] = part[:, pl.ds(pl.multiple_of(q * 8, 8), 8), :]
    span1 = got1.at[pl.ds(0, NXY - 1)]
    pltpu.make_async_copy(span1, span1, b_sem.at[1]).wait()
    pltpu.make_async_copy(span1, span1, b_sem.at[0]).wait()
    acc = got1[0]
    for k in range(1, NXY):
        acc = acc + got1[k]
    col[...] = acc

    def send2(k, carry):
        other, device = z_peer(k)
        pltpu.make_async_remote_copy(
            col.at[other], got2.at[z],
            c_sem.at[0], c_sem.at[1], device_id=device, device_id_type=MESH).start()
        return carry

    lax.fori_loop(1, NZ, send2, 0)
    got2[z] = col[z]
    span2 = got2.at[pl.ds(0, NZ - 1)]
    pltpu.make_async_copy(span2, span2, c_sem.at[1]).wait()
    pltpu.make_async_copy(span2, span2, c_sem.at[0]).wait()
    acc = got2[0]
    for k in range(1, NZ):
        acc = acc + got2[k]

    mine[z] = acc

    def send3(k, carry):
        _, device = z_peer(k)
        pltpu.make_async_remote_copy(
            mine.at[z], mine.at[z],
            d_sem.at[0], d_sem.at[1], device_id=device, device_id_type=MESH).start()
        return carry

    lax.fori_loop(1, NZ, send3, 0)
    span3 = mine.at[pl.ds(0, NZ - 1)]
    pltpu.make_async_copy(span3, span3, d_sem.at[1]).wait()
    pltpu.make_async_copy(span3, span3, d_sem.at[0]).wait()

    rows = pl.ds(pl.multiple_of(q * 8, 8), 8)

    def send4(k, carry):
        _, device = xy_peer(k)
        pltpu.make_async_remote_copy(
            mine, total.at[own, rows],
            e_sem.at[0], e_sem.at[1], device_id=device, device_id_type=MESH).start()
        return carry

    lax.fori_loop(1, NXY, send4, 0)
    total[own, rows, :] = mine[...]
    span4 = got1.at[pl.ds(0, NXY - 1)]
    pltpu.make_async_copy(span4, span4, e_sem.at[1]).wait()
    pltpu.make_async_copy(span4, span4, e_sem.at[0]).wait()

    pair1 = pltpu.make_async_remote_copy(
        total.at[own], total.at[own], f_sem.at[0], f_sem.at[1], device_id=partner, device_id_type=MESH)
    pair1.start()
    exchange_wait(slots, recv, sems, zpair)
    pair1.wait()


def build_halo(pad, x_ref, recv, slot_ref, low, high, lkeep, hkeep, faces):
    for a in (0, 5):
        for b in (0, 5):
            for c in range(6):
                pad[a, b, c] = jnp.zeros((BP, CH), BF)
                if 0 < c < 5:
                    pad[a, c, b] = jnp.zeros((BP, CH), BF)
                    pad[c, a, b] = jnp.zeros((BP, CH), BF)
    for i in range(4):
        for j in range(4):
            for k in range(4):
                pad[i + 1, j + 1, k + 1] = x_ref[4 * i + j, k]
            pad[i + 1, j + 1, 0] = (low[4 * i + j].astype(F32) * lkeep[...]).astype(BF)
            pad[i + 1, j + 1, 5] = (high[4 * i + j].astype(F32) * hkeep[...]).astype(BF)
    for side in range(4):
        faces[side, BD * 16 :, :] = jnp.zeros(((BP - BD) * 16, CH), F32)

        def body(b, carry):
            slot = slot_ref[side * BD + b]
            safe = jnp.maximum(slot, 0)
            tile = recv[pl.ds(pl.multiple_of(safe * 16, 16), 16), :].astype(F32)
            faces[side, pl.ds(pl.multiple_of(b * 16, 16), 16), :] = jnp.where(slot >= 0, tile, 0.0)
            return carry

        lax.fori_loop(0, BD, body, 0)
        for a in range(4):
            for b in range(4):
                slab = faces[side, pl.ds(4 * a + b, BP, stride=16), :].astype(BF)
                if side < 2:
                    pad[5 * side, a + 1, b + 1] = slab
                else:
                    pad[a + 1, 5 * (side - 2), b + 1] = slab


def conv_plane(pad, w_ref, plane):
    acc = None
    for o1 in range(3):
        for o2 in range(3):
            lhs = jnp.concatenate(
                [pad[plane + o1, o2 : o2 + 4, o3 : o3 + 4].reshape(16 * BP, CH) for o3 in range(3)],
                axis=1)
            tap = 9 * o1 + 3 * o2
            term = jnp.dot(lhs, w_ref[tap * CH : (tap + 3) * CH, :], preferred_element_type=F32)
            acc = term if acc is None else acc + term
    return acc


def forward_kernel(x_ref, recv, low, high, recv_slot, send_slot, lkeep, hkeep, w_ref, cot, occ,
                   out, g_ref, slots, grad, pad, faces, rows, outs, gt):
    build_halo(pad, x_ref, recv, recv_slot, low, high, lkeep, hkeep, faces)
    rows[0 : BD * VOX, :] = cot[...].astype(F32)
    rows[BD * VOX :, :] = jnp.zeros((BP * VOX - BD * VOX, CH), F32)

    def plane_body(plane, carry):
        pre = conv_plane(pad, w_ref, plane)
        mask = occ[plane]
        for t in range(16):
            u = pre[t * BP : (t + 1) * BP, :]
            s = 1.0 / (1.0 + jnp.exp(-u))
            m = mask[:, t : t + 1]
            f = x_ref[4 * plane + t // 4, t % 4].astype(F32)
            c = rows[pl.ds(16 * plane + t, BP, stride=VOX), :]
            outs[pl.ds(16 * plane + t, BP, stride=VOX), :] = f + m * (u * s)
            g_ref[4 * plane + t // 4, t % 4] = (c * m * s * (1.0 + u * (1.0 - s))).astype(BF)
        return carry

    lax.fori_loop(0, 4, plane_body, 0)
    out[...] = outs[0 : BD * VOX, :].astype(BF)
    fill_faces(lambda v: g_ref[v // 4, v % 4].astype(F32), faces)
    pack_slots(faces, send_slot, slots)
    for k in range(16):
        gt[:, 128 * k : 128 * (k + 1)] = g_ref[k].reshape(128, CH).T

    def tap_body(n, carry):
        o1 = n // 3
        o2 = lax.rem(n, 3)
        rhs = jnp.concatenate(
            [pad[pl.ds(o1, 4), pl.ds(o2, 4), o3 : o3 + 4].reshape(VOX * BP, CH) for o3 in range(3)],
            axis=1)
        res = jnp.dot(gt[...], rhs, preferred_element_type=F32)
        for o3 in range(3):
            grad[3 * n + o3] = res[:, CH * o3 : CH * (o3 + 1)].T
        return carry

    lax.fori_loop(0, 9, tap_body, 0)
    for t in range(TAPS, TPAD):
        grad[t] = jnp.zeros((CH, CH), F32)


def backward_kernel(g_ref, recv, low, high, recv_slot, lkeep, hkeep, w_ref, cot, out, pad, faces, rows, outs):
    build_halo(pad, g_ref, recv, recv_slot, low, high, lkeep, hkeep, faces)
    rows[0 : BD * VOX, :] = cot[...].astype(F32)
    rows[BD * VOX :, :] = jnp.zeros((BP * VOX - BD * VOX, CH), F32)

    def plane_body(plane, carry):
        back = conv_plane(pad, w_ref, plane)
        for t in range(16):
            c = rows[pl.ds(16 * plane + t, BP, stride=VOX), :]
            outs[pl.ds(16 * plane + t, BP, stride=VOX), :] = c + back[t * BP : (t + 1) * BP, :]
        return carry

    lax.fori_loop(0, 4, plane_body, 0)
    out[...] = outs[0 : BD * VOX, :].astype(BF)


def slot_tables(neighbors, me):
    linked = neighbors.T[:4].reshape(4 * BD)
    present = linked >= 0
    owner = jnp.where(present, linked // (BD * SLB), -1)
    position = linked % BD
    key = jnp.arange(4 * BD, dtype=jnp.int32)
    side = key // BD
    wanted = (side + 1 - 2 * (side % 2)) * BD + position
    same = owner[:, None] == owner[None, :]
    send_rank = jnp.sum(same & (key[None, :] < key[:, None]), axis=1, dtype=jnp.int32)
    recv_rank = jnp.sum(same & (wanted[None, :] < wanted[:, None]), axis=1, dtype=jnp.int32)
    send_slot = jnp.where(present, owner * 2 + send_rank, 2 * me)
    recv_slot = jnp.where(present, owner * 2 + recv_rank, -1)
    return send_slot, recv_slot


def shards(features, weight, cotangent, occupancy, neighbors):
    me = lax.axis_index("region")
    send_slot, recv_slot = slot_tables(neighbors, me)
    keep = (neighbors[:, 4:6] >= 0).astype(F32)
    keep = jnp.pad(keep, ((0, BP - BD), (0, 0)))
    lkeep, hkeep = keep[:, 0:1], keep[:, 1:2]
    occ = jnp.pad(occupancy.astype(F32), ((0, BP - BD), (0, 0))).reshape(BP, 4, 16).swapaxes(0, 1)
    feat = features.reshape(BD * VOX, CH)
    cot = cotangent.reshape(BD * VOX, CH)
    w = weight.reshape(TAPS * CH, CH)
    flipped = jnp.swapaxes(weight[::-1], 1, 2).reshape(TAPS * CH, CH)

    vox = vmem((16, 4, BP, CH), BF)
    slot_shape = vmem((SLOTS * 16, CH), BF)
    face_shape = vmem((16, BP, CH), BF)
    x_major, slots = pl.pallas_call(
        pack_kernel,
        out_shape=(vmem((VOX, BP, CH), BF), slot_shape),
        in_specs=[IN_VMEM, IN_SMEM],
        out_specs=(IN_VMEM, IN_VMEM),
        scratch_shapes=[pltpu.VMEM((BP * VOX, CH), F32), pltpu.VMEM((4, BP * 16, CH), F32)],
        compiler_params=params(),
        name="pack_features",
    )(feat, send_slot)
    x_major = x_major.reshape(16, 4, BP, CH)

    dma = pltpu.SemaphoreType.DMA
    recv, low, high = pl.pallas_call(
        first_exchange,
        out_shape=(slot_shape, face_shape, face_shape),
        in_specs=[IN_VMEM] * 2,
        out_specs=(IN_VMEM,) * 3,
        scratch_shapes=[dma, dma, dma((2,)), dma((2,))],
        compiler_params=params(collective_id=0, has_side_effects=True),
        name="exchange_features",
    )(slots, x_major)

    output, g_major, g_slots, grad = pl.pallas_call(
        forward_kernel,
        out_shape=(vmem((BD * VOX, CH), BF), vox, slot_shape, vmem((TPAD, CH, CH), F32)),
        in_specs=[IN_VMEM] * 4 + [IN_SMEM] * 2 + [IN_VMEM] * 5,
        out_specs=(IN_VMEM,) * 4,
        scratch_shapes=[
            pltpu.VMEM((6, 6, 6, BP, CH), BF),
            pltpu.VMEM((4, BP * 16, CH), F32),
            pltpu.VMEM((BP * VOX, CH), F32),
            pltpu.VMEM((BP * VOX, CH), F32),
            pltpu.VMEM((CH, BP * VOX), BF),
        ],
        compiler_params=params(),
        name="forward",
    )(x_major, recv, low, high, recv_slot, send_slot, lkeep, hkeep, w, cot, occ)

    recv2, low2, high2, total = pl.pallas_call(
        second_exchange,
        out_shape=(slot_shape, face_shape, face_shape, vmem((TPAD, CH, CH), F32)),
        in_specs=[IN_VMEM] * 3,
        out_specs=(IN_VMEM,) * 4,
        scratch_shapes=[
            pltpu.VMEM((HALF_T, CH, CH), F32),
            pltpu.VMEM((HALF_T, 8, CH), F32),
            pltpu.VMEM((HALF_T, 8, CH), F32),
            pltpu.VMEM((HALF_T, CH, CH), F32),
            pltpu.VMEM((NXY, HALF_T, 8, CH), F32),
            pltpu.VMEM((NZ, 8, CH), F32),
            dma, dma, dma((2,)), dma((2,)),
        ] + [dma((2,))] * 6,
        compiler_params=params(collective_id=1, has_side_effects=True),
        name="exchange_gradients",
    )(g_slots, g_major, grad)

    input_grad = pl.pallas_call(
        backward_kernel,
        out_shape=vmem((BD * VOX, CH), BF),
        in_specs=[IN_VMEM] * 4 + [IN_SMEM] + [IN_VMEM] * 4,
        out_specs=IN_VMEM,
        scratch_shapes=[
            pltpu.VMEM((6, 6, 6, BP, CH), BF),
            pltpu.VMEM((4, BP * 16, CH), F32),
            pltpu.VMEM((BP * VOX, CH), F32),
            pltpu.VMEM((BP * VOX, CH), F32),
        ],
        compiler_params=params(),
        name="backward",
    )(g_major, recv2, low2, high2, recv_slot, lkeep, hkeep, flipped, cot)

    weight_grad = total[:TAPS] * (BD * REG * SLB * float(VOX)) ** -0.5
    return output.reshape(features.shape), input_grad.reshape(features.shape), weight_grad


def solution(mesh):
    return jax.shard_map(
        shards,
        mesh=mesh,
        in_specs=(
            P(("region", "slab"), None, None, None, None),
            P(),
            P(("region", "slab"), None, None, None, None),
            P(("region", "slab"), None),
            P(("region", "slab"), None),
        ),
        out_specs=(
            P(("region", "slab"), None, None, None, None),
            P(("region", "slab"), None, None, None, None),
            P(),
        ),
        check_vma=False,
    )
```

time: 661 us -> 195 us (0.30)
  waiting for transfers between devices: 518 us -> 0 us
  Pallas kernels: 0 us -> 184 us
  matrix products: 43 us -> 0 us
  starting transfers between devices: 35.7 us -> 0 us
  local copies, waits for them, and re-layouts: 29.3 us -> 6.22 us
  between operations: 15.7 us -> 0.74 us
  other arithmetic: 12.5 us -> 3.18 us
    psum x1 -> x0, waiting for transfers between devices: 466 us -> none  [shards(): summed = lax.psum(local_grad, ('region', 'slab'))]
    pallas_call x0 -> x5, Pallas kernels: none -> 184 us  [the longest x1 91.6 us: shards(): pl.pallas_call(second_exchange, out_shape=(slot_shape, face_shape, face_s...]
    all_to_all x2 -> x0, waiting for transfers between devices: 45.5 us -> none  [brick_pads(): lax.all_to_all(outgoing, 'region', split_axis=0, concat_axis=0, tiled=True)]
    dot_general x85 -> x0, matrix products: 43 us -> none  [the longest x27 27.3 us: shards(): jnp.einsum('rc,rd->cd', window, flat_grad, preferred_element_type=jnp.flo...]
    all_to_all x2 -> x0, starting transfers between devices: 28.2 us -> none  [brick_pads(): lax.all_to_all(outgoing, 'region', split_axis=0, concat_axis=0, tiled=True)]
    slice x63 -> x2, local copies, waits for them, and re-layouts: 16 us -> 0.76 us  [the longest x1 0.69 us: shards(): keep = (neighbors[:, 4:6] >= 0).astype(F32)]
    ppermute x4 -> x0, starting transfers between devices: 7.47 us -> none  [the longest x2 4.88 us: with_halo(): lax.ppermute(lax.slice_in_dim(block, 0, width, axis=dim), axis, backward)]
  transfers between devices with their start and end apart: 7 -> 0, of which waited for: 4 -> 0; matrix products, arithmetic and copies ran while one was open for 5% -> 0% of each run, Pallas kernels for 0% -> 0%
where the time goes in v1:
time: 195 us; the launch traced here: 194 us
  Pallas kernels  184 us (94%)
  local copies, waits for them, and re-layouts  6.22 us (3%)
  other arithmetic  3.18 us (2%)
    pallas_call x1, Pallas kernels, shards(): pl.pallas_call(second_exchange, out_shape=(slot_shape, face_shape, face_s...  91.6 us
    pallas_call x1, Pallas kernels, shards(): pl.pallas_call(first_exchange, out_shape=(slot_shape, face_shape, face_sh...  65.1 us
    pallas_call x1, Pallas kernels, shards(): pl.pallas_call(forward_kernel, out_shape=(vmem((BD * VOX, CH), BF), vox,...  16.1 us
    pallas_call x1, Pallas kernels, shards(): pl.pallas_call(backward_kernel, out_shape=vmem((BD * VOX, CH), BF), in_sp...  8.39 us

profile of v1, /device:TPU:25, one launch (start us, length us, event | category | flops | bytes accessed | tf_op | source)
XLA Modules:
  0.0 194.0 jit_solution(4712537023319120)
XLA Ops:
  0.6 0.0 copy-start
  0.6 0.0 copy-start.1
  0.7 0.8 fusion
  1.5 0.1 ge.27
  1.5 0.7 slice_divide_fusion
  2.2 0.1 rem.78
  2.3 0.1 and.65
  2.4 0.1 div.30
  2.5 0.2 convert_reduce_fusion
  2.7 0.0 copy-start.3
  2.7 1.0 copy-done.3
  3.7 0.0 copy-start.5
  3.7 2.7 %pack_features.1 = (bf16[64,32,128]{2,1,0:T(8,128)(2,1)S(1)}, bf16[4096,128]{1,0:T(8,128)(2,1)S(1)}) custom-call(bf16[1664,128]{1,0:T(8,128)(2,1)S(1)} %bitcast.18, s32[104]{0:T(128)S(1)} %get-tuple-element.38.slot_ref.send_slot), custom_call_target="tpu_custom_call" | custom-call | tf_op jit(solution)/shard_map/pack_features/pallas_call | solution.py:395
  6.4 65.1 %exchange_features.1 = (bf16[4096,128]{1,0:T(8,128)(2,1)S(1)}, bf16[16,32,128]{2,1,0:T(8,128)(2,1)S(1)}, bf16[16,32,128]{2,1,0:T(8,128)(2,1)S(1)}) custom-call(bf16[4096,128]{1,0:T(8,128)(2,1)S(1)} %get-tuple-element.17.slots, bf16[16,4,32,128]{3,2,1,0:T(8,128)(2,1)S(1)} %bitcast.14), custom_call_target="tpu_custom_call" | custom-call | tf_op jit(solution)/shard_map/exchange_features/pallas_call | solution.py:407
  71.5 0.0 copy-start.2
  71.5 1.0 copy-done.2
  72.5 0.7 slice.16
  73.2 0.1 copy.22
  73.3 0.1 fusion.6
  73.4 0.0 copy-done.5
  73.4 0.1 copy.23
  73.5 0.1 copy.20
  73.6 0.0 copy-done
  73.6 0.0 copy-done.1
  73.6 16.1 %forward.1 = (bf16[1664,128]{1,0:T(8,128)(2,1)}, bf16[16,4,32,128]{3,2,1,0:T(8,128)(2,1)S(1)}, bf16[4096,128]{1,0:T(8,128)(2,1)S(1)}, f32[32,128,128]{2,1,0:T(8,128)}) custom-call(bf16[16,4,32,128]{3,2,1,0:T(8,128)(2,1)S(1)} %bitcast.15, bf16[4096,128]{1,0:T(8,128)(2,1)} %copy-done.2, bf16[16,32,128]{2,1,0:T(8,128)(2,1)S(1)} %get-tuple-element.19.low, ...), custom_call_target="tpu_custom_call" | custom-call | tf_op jit(solution)/shard_map/forward/pallas_call | solution.py:417
  89.7 91.6 %exchange_gradients.1 = (bf16[4096,128]{1,0:T(8,128)(2,1)S(1)}, bf16[16,32,128]{2,1,0:T(8,128)(2,1)S(1)}, bf16[16,32,128]{2,1,0:T(8,128)(2,1)S(1)}, f32[32,128,128]{2,1,0:T(8,128)}) custom-call(bf16[4096,128]{1,0:T(8,128)(2,1)S(1)} %get-tuple-element.23.slots, bf16[16,4,32,128]{3,2,1,0:T(8,128)(2,1)S(1)} %get-tuple-element.22.x_ref.g_ref, ...), custom_call_target="tpu_custom_call" | custom-call | tf_op jit(solution)/shard_map/exchange_gradients/pallas_call | solution.py:433
  181.3 1.0 reverse_bitcast_fusion
  182.3 1.9 copy.21
  184.1 0.0 copy-start.4
  184.2 8.4 %backward.1 = bf16[1664,128]{1,0:T(8,128)(2,1)} custom-call(bf16[16,4,32,128]{3,2,1,0:T(8,128)(2,1)S(1)} %get-tuple-element.22.x_ref.g_ref, bf16[4096,128]{1,0:T(8,128)(2,1)S(1)} %get-tuple-element.25.recv, bf16[16,32,128]{2,1,0:T(8,128)(2,1)S(1)} %get-tuple-element.26.low, bf16[16,32,128]{2,1,0:T(8,128)(2,1)S(1)} %get-tuple-element.27.high, ...), custom_call_target="tpu_custom_call" | custom-call | tf_op jit(solution)/shard_map/backward/pallas_call | solution.py:451
  192.5 0.0 copy-done.4
  192.5 1.4 slice_multiply_fusion
  (6 shorter events, 0.1 us)
Async XLA Ops:
  0.6 72.9 %copy-start = (bf16[27,128,128]{2,1,0:T(8,128)(2,1)S(1)}, bf16[27,128,128]{2,1,0:T(8,128)(2,1)}, u32[]{:S(2)}) copy-start(bf16[27,128,128]{2,1,0:T(8,128)(2,1)} %param.6) | copy-start | bytes 2654212
  0.6 72.9 %copy-start.1 = (bf16[26,4,4,4,128]{4,3,2,1,0:T(4,128)(2,1)S(1)}, bf16[26,4,4,4,128]{4,3,2,1,0:T(4,128)(2,1)}, u32[]{:S(2)}) copy-start(bf16[26,4,4,4,128]{4,3,2,1,0:T(4,128)(2,1)} %param.7) | copy-start | bytes 1277956
  2.7 1.0 copy-start.3
  3.7 69.7 %copy-start.5 = (s32[26,64]{1,0:T(8,128)S(1)}, s32[26,64]{1,0:T(8,128)}, u32[]{:S(2)}) copy-start(s32[26,64]{1,0:T(8,128)} %param.8) | copy-start | bytes 19972
  71.5 1.0 copy-start.2
  184.1 8.4 %copy-start.4 = (f32[32,128,128]{2,1,0:T(8,128)S(1)}, f32[32,128,128]{2,1,0:T(8,128)}, u32[]{:S(2)}) copy-start(f32[32,128,128]{2,1,0:T(8,128)} %get-tuple-element.28) | copy-start | bytes 6291460

commit v2 on v0

v2 whole, which is shorter than its diff:
```python
import functools

import jax
import jax.numpy as jnp
from jax import lax
from jax.experimental import pallas as pl
from jax.experimental.pallas import tpu as pltpu
from jax.sharding import PartitionSpec as P

MESH = pl.DeviceIdType.MESH
BF = jnp.bfloat16
F32 = jnp.float32

CH = 128
BD = 26
BP = 32
VOX = 64
REG = 128
SLB = 4
NX, NZ, NCORE = 4, 16, 2
NXY = NX * SLB
SLOTS = 2 * REG
TAPS = 27
HALF_T = 14
TPAD = 2 * HALF_T
CUTS = (1, 50, 70, 80, 90, REG)
VMEM_LIMIT = 50 * 1024 * 1024


def params(**kw):
    return pltpu.CompilerParams(vmem_limit_bytes=VMEM_LIMIT, **kw)


def vmem(shape, dtype):
    return jax.ShapeDtypeStruct(shape, dtype)


IN_VMEM = pl.BlockSpec(memory_space=pltpu.VMEM)
IN_SMEM = pl.BlockSpec(memory_space=pltpu.SMEM)
IN_ANY = pl.BlockSpec(memory_space=pl.ANY)


def face_voxels(side):
    if side == 0:
        return [4 * a + b for a in range(4) for b in range(4)]
    if side == 1:
        return [48 + 4 * a + b for a in range(4) for b in range(4)]
    if side == 2:
        return [16 * a + b for a in range(4) for b in range(4)]
    return [16 * a + 12 + b for a in range(4) for b in range(4)]


def fill_faces(slabs, faces):
    faces = faces.reshape(4, BP * 16, CH)
    for side in range(4):
        for t, v in enumerate(face_voxels(side)):
            faces[side, pl.ds(t, BP, stride=16), :] = slabs(v)


def zero_rim(pad):
    for a in (0, 5):
        for b in (0, 5):
            for c in range(6):
                pad[a, b, c] = jnp.zeros((BP, CH), BF)
                if 0 < c < 5:
                    pad[a, c, b] = jnp.zeros((BP, CH), BF)
                    pad[c, a, b] = jnp.zeros((BP, CH), BF)


def build_halo(pad, recv, slot_ref, low, high, lkeep, hkeep, faces):
    for i in range(4):
        for j in range(4):
            pad[i + 1, j + 1, 0] = (low[i, j].astype(F32) * lkeep[...]).astype(BF)
            pad[i + 1, j + 1, 5] = (high[i, j].astype(F32) * hkeep[...]).astype(BF)
    for side in range(4):

        def body(b, carry):
            faces[side * BP + b] = recv[slot_ref[side * BP + b]].astype(F32)
            return carry

        lax.fori_loop(0, BP, body, 0)
    faces = faces.reshape(4, BP * 16, CH)
    for side in range(4):
        for a in range(4):
            for b in range(4):
                slab = faces[side, pl.ds(4 * a + b, BP, stride=16), :].astype(BF)
                if side < 2:
                    pad[5 * side, a + 1, b + 1] = slab
                else:
                    pad[a + 1, 5 * (side - 2), b + 1] = slab


def conv_plane(pad, w_ref, plane):
    acc = None
    for o1 in range(3):
        for o2 in range(3):
            lhs = jnp.concatenate(
                [pad[plane + o1, o2 : o2 + 4, o3 : o3 + 4].reshape(16 * BP, CH) for o3 in range(3)],
                axis=1)
            tap = 9 * o1 + 3 * o2
            term = jnp.dot(lhs, w_ref[tap * CH : (tap + 3) * CH, :], preferred_element_type=F32)
            acc = term if acc is None else acc + term
    return acc


def place(axis_region, slab):
    core = lax.rem(axis_region, NCORE)
    z = lax.rem(axis_region // NCORE, NZ)
    x = axis_region // (NZ * NCORE)
    return x, z, core, x * SLB + slab


def pack_and_send(me, slab, lo, hi, faces, source_ref, slots, recv, send_sem, recv_sem):
    def send(k, carry):
        peer = lax.rem(me + k, REG)
        for half in range(2):
            source = source_ref[2 * peer + half]
            slots[2 * peer + half] = faces[source].astype(BF)
        pltpu.make_async_remote_copy(
            slots.at[pl.ds(2 * peer, 2)],
            recv.at[pl.ds(2 * me, 2)],
            send_sem, recv_sem,
            device_id={"region": peer, "slab": slab}, device_id_type=MESH,
        ).start()
        return carry

    lax.fori_loop(lo, hi, send, 0)


def slab_copies(me, slab, pad, low, high, z_send, z_recv):
    up = lax.rem(slab + 1, SLB)
    down = lax.rem(slab + SLB - 1, SLB)
    to_up = pltpu.make_async_remote_copy(
        pad.at[1:5, 1:5, 4], low, z_send.at[0], z_recv.at[0],
        device_id={"region": me, "slab": up}, device_id_type=MESH)
    to_down = pltpu.make_async_remote_copy(
        pad.at[1:5, 1:5, 1], high, z_send.at[1], z_recv.at[1],
        device_id={"region": me, "slab": down}, device_id_type=MESH)
    return to_up, to_down


def wait_bytes(ref, sem):
    pltpu.make_async_copy(ref, ref, sem).wait()


def section_kernel(feat, cot, w_ref, occ, lkeep, hkeep, source_ref, recv_slot,
                   out, input_grad, total,
                   padf, padg, wflip, rows, crows, outs, faces, slots, slots2, recv, recv2,
                   low, high, low2, high2, gt, grad,
                   part, col, mine, half_bf, all_bf, got0, got1, got2,
                   s1, r1, zs1, zr1, s2, r2, zs2, zr2, a_sem, b_sem, c_sem, d_sem, e_sem, f_sem):
    me = lax.axis_index("region")
    slab = lax.axis_index("slab")
    x, z, core, q = place(me, slab)

    def region_of(xx, zz, cc):
        return (xx * NZ + zz) * NCORE + cc

    def xy_peer(k):
        other = lax.rem(q + k, NXY)
        return other, {"region": region_of(other // SLB, z, core), "slab": lax.rem(other, SLB)}

    def z_peer(k):
        other = lax.rem(z + k, NZ)
        return other, {"region": region_of(x, other, core), "slab": slab}

    partner = {"region": region_of(x, z, 1 - core), "slab": slab}

    barrier = pltpu.get_barrier_semaphore()

    def greet(k, carry):
        pl.semaphore_signal(
            barrier, inc=1, device_id={"region": lax.rem(me + k, REG), "slab": slab},
            device_id_type=MESH)
        return carry

    lax.fori_loop(1, REG, greet, 0)

    def greet_slabs(k, carry):
        s = lax.rem(slab + 1 + lax.rem(k, SLB - 1), SLB)
        pl.semaphore_signal(
            barrier, inc=1, device_id={"region": region_of(k // (SLB - 1), z, core), "slab": s},
            device_id_type=MESH)
        return carry

    lax.fori_loop(0, NX * (SLB - 1), greet_slabs, 0)

    rows[0 : BD * VOX, :] = feat[...].astype(F32)
    rows[BD * VOX :, :] = jnp.zeros((BP * VOX - BD * VOX, CH), F32)
    for v in range(VOX):
        padf[v // 16 + 1, v // 4 % 4 + 1, v % 4 + 1] = rows[pl.ds(v, BP, stride=VOX), :].astype(BF)
    fill_faces(lambda v: rows[pl.ds(v, BP, stride=VOX), :], faces)

    pl.semaphore_wait(barrier, REG - 1 + NX * (SLB - 1))
    pair = slab_copies(me, slab, padf, low, high, zs1, zr1)
    for copy in pair:
        copy.start()
    pack_and_send(me, slab, 1, REG, faces, source_ref, slots, recv, s1, r1)

    zero_rim(padf)
    zero_rim(padg)
    for t in range(TAPS):
        wflip[t * CH : (t + 1) * CH, :] = w_ref[(TAPS - 1 - t) * CH : (TAPS - t) * CH, :].T
    crows[0 : BD * VOX, :] = cot[...].astype(F32)
    crows[BD * VOX :, :] = jnp.zeros((BP * VOX - BD * VOX, CH), F32)
    for t in range(TAPS, TPAD):
        grad[t] = jnp.zeros((CH, CH), F32)
    for buffer in (recv, recv2):
        for half in range(2):
            buffer[2 * me + half] = jnp.zeros((16, CH), BF)

    for copy in pair:
        copy.wait()
    peers = pl.ds(0, 2 * (REG - 1))
    wait_bytes(recv.at[peers], r1)
    wait_bytes(slots.at[peers], s1)

    build_halo(padf, recv, recv_slot, low, high, lkeep, hkeep, faces)

    def plane_body(plane, carry):
        pre = conv_plane(padf, w_ref, plane)
        mask = occ[plane]
        for t in range(16):
            u = pre[t * BP : (t + 1) * BP, :]
            s = 1.0 / (1.0 + jnp.exp(-u))
            m = mask[:, t : t + 1]
            f = padf[plane + 1, t // 4 + 1, t % 4 + 1].astype(F32)
            c = crows[pl.ds(16 * plane + t, BP, stride=VOX), :]
            outs[pl.ds(16 * plane + t, BP, stride=VOX), :] = f + m * (u * s)
            padg[plane + 1, t // 4 + 1, t % 4 + 1] = (c * m * s * (1.0 + u * (1.0 - s))).astype(BF)
        return carry

    lax.fori_loop(0, 4, plane_body, 0)
    fill_faces(lambda v: padg[v // 16 + 1, v // 4 % 4 + 1, v % 4 + 1].astype(F32), faces)
    pair = slab_copies(me, slab, padg, low2, high2, zs2, zr2)
    for copy in pair:
        copy.start()

    def send_faces(n):
        pack_and_send(me, slab, CUTS[n], CUTS[n + 1], faces, source_ref, slots2, recv2, s2, r2)

    send_faces(0)

    for i in range(4):
        for j in range(4):
            gt[:, 128 * (4 * i + j) : 128 * (4 * i + j + 1)] = (
                padg[i + 1, j + 1, 1:5].reshape(4 * BP, CH).T)

    def tap_body(n, carry):
        o1 = n // 3
        o2 = lax.rem(n, 3)
        rhs = jnp.concatenate(
            [padf[pl.ds(o1, 4), pl.ds(o2, 4), o3 : o3 + 4].reshape(VOX * BP, CH) for o3 in range(3)],
            axis=1)
        res = jnp.dot(gt[...], rhs, preferred_element_type=F32)
        for o3 in range(3):
            grad[3 * n + o3] = res[:, CH * o3 : CH * (o3 + 1)].T
        return carry

    lax.fori_loop(0, 9, tap_body, 0)

    own = pl.ds(core * HALF_T, HALF_T)
    other_half = pl.ds((1 - core) * HALF_T, HALF_T)
    pair0 = pltpu.make_async_remote_copy(
        grad.at[other_half], got0, a_sem.at[0], a_sem.at[1], device_id=partner, device_id_type=MESH)
    pair0.start()
    out[...] = outs[0 : BD * VOX, :].astype(BF)
    pair0.wait()

    def add_pair(t, carry):
        part[t] = grad[core * HALF_T + t] + got0[t]
        return carry

    lax.fori_loop(0, HALF_T, add_pair, 0)

    def send1(k, carry):
        other, device = xy_peer(k)
        pltpu.make_async_remote_copy(
            part.at[:, pl.ds(pl.multiple_of(other * 8, 8), 8)], got1.at[q],
            b_sem.at[0], b_sem.at[1], device_id=device, device_id_type=MESH).start()
        return carry

    lax.fori_loop(1, NXY, send1, 0)
    send_faces(1)
    got1[q] = part[:, pl.ds(pl.multiple_of(q * 8, 8), 8), :]
    span1 = got1.at[pl.ds(0, NXY - 1)]
    wait_bytes(span1, b_sem.at[1])
    wait_bytes(span1, b_sem.at[0])
    acc = got1[0]
    for k in range(1, NXY):
        acc = acc + got1[k]
    col[...] = acc

    def send2(k, carry):
        other, device = z_peer(k)

        @pl.when(other < HALF_T)
        def _():
            pltpu.make_async_remote_copy(
                col.at[other], got2.at[z],
                c_sem.at[0], c_sem.at[1], device_id=device, device_id_type=MESH).start()

        return carry

    lax.fori_loop(1, NZ, send2, 0)
    send_faces(2)

    @pl.when(z < HALF_T)
    def _():
        got2[z] = col[z]
        wait_bytes(got2.at[pl.ds(0, NZ - 1)], c_sem.at[1])
        wait_bytes(got2.at[pl.ds(0, HALF_T - 1)], c_sem.at[0])
        acc = got2[0]
        for k in range(1, NZ):
            acc = acc + got2[k]
        mine[z] = acc

    @pl.when(z >= HALF_T)
    def _():
        wait_bytes(got2.at[pl.ds(0, HALF_T)], c_sem.at[0])

    @pl.when(z < HALF_T)
    def _():
        def send3(k, carry):
            _, device = z_peer(k)
            pltpu.make_async_remote_copy(
                mine.at[z], mine.at[z],
                d_sem.at[0], d_sem.at[1], device_id=device, device_id_type=MESH).start()
            return carry

        lax.fori_loop(1, NZ, send3, 0)

    send_faces(3)

    @pl.when(z < HALF_T)
    def _():
        wait_bytes(mine.at[pl.ds(0, HALF_T - 1)], d_sem.at[1])
        wait_bytes(got2.at[pl.ds(0, NZ - 1)], d_sem.at[0])

    @pl.when(z >= HALF_T)
    def _():
        wait_bytes(mine.at[pl.ds(0, HALF_T)], d_sem.at[1])

    half_bf[...] = mine[...].reshape(HALF_T * 8, CH).astype(BF)

    def send4(k, carry):
        _, device = xy_peer(k)
        pltpu.make_async_remote_copy(
            half_bf, all_bf.at[core, q],
            e_sem.at[0], e_sem.at[1], device_id=device, device_id_type=MESH).start()
        return carry

    lax.fori_loop(1, NXY, send4, 0)
    send_faces(4)
    all_bf[core, q] = half_bf[...]
    span4 = all_bf.at[0, pl.ds(0, NXY - 1)]
    wait_bytes(span4, e_sem.at[1])
    wait_bytes(span4, e_sem.at[0])

    pair1 = pltpu.make_async_remote_copy(
        all_bf.at[core], all_bf.at[core], f_sem.at[0], f_sem.at[1], device_id=partner, device_id_type=MESH)
    pair1.start()
    pair1.wait()
    for c in range(NCORE):
        for k in range(NXY):
            total[HALF_T * c : HALF_T * (c + 1), 8 * k : 8 * k + 8, :] = (
                all_bf[c, k].astype(F32).reshape(HALF_T, 8, CH))

    for copy in pair:
        copy.wait()
    wait_bytes(recv2.at[peers], r2)
    wait_bytes(slots2.at[peers], s2)
    build_halo(padg, recv2, recv_slot, low2, high2, lkeep, hkeep, faces)

    def back_body(plane, carry):
        back = conv_plane(padg, wflip, plane)
        for t in range(16):
            c = crows[pl.ds(16 * plane + t, BP, stride=VOX), :]
            outs[pl.ds(16 * plane + t, BP, stride=VOX), :] = c + back[t * BP : (t + 1) * BP, :]
        return carry

    lax.fori_loop(0, 4, back_body, 0)
    input_grad[...] = outs[0 : BD * VOX, :].astype(BF)


def slot_tables(neighbors, me):
    linked = neighbors.T[:4].reshape(4 * BD)
    present = linked >= 0
    owner = jnp.where(present, linked // (BD * SLB), -1)
    position = linked % BD
    key = jnp.arange(4 * BD, dtype=jnp.int32)
    side = key // BD
    wanted = (side + 1 - 2 * (side % 2)) * BD + position
    same = owner[:, None] == owner[None, :]
    send_rank = jnp.sum(same & (key[None, :] < key[:, None]), axis=1, dtype=jnp.int32)
    recv_rank = jnp.sum(same & (wanted[None, :] < wanted[:, None]), axis=1, dtype=jnp.int32)
    send_slot = jnp.where(present, owner * 2 + send_rank, -1)
    recv_slot = jnp.where(present, owner * 2 + recv_rank, 2 * me)
    recv_slot = jnp.pad(recv_slot.reshape(4, BD), ((0, 0), (0, BP - BD)), constant_values=0)
    recv_slot = jnp.where(jnp.arange(BP)[None, :] < BD, recv_slot, 2 * me).reshape(4 * BP)
    slot = jnp.arange(SLOTS, dtype=jnp.int32)
    face = side * BP + key - side * BD
    source = jnp.sum(jnp.where(send_slot[None, :] == slot[:, None], face[None, :], 0), axis=1, dtype=jnp.int32)
    return source, recv_slot


def shards(features, weight, cotangent, occupancy, neighbors):
    source, recv_slot = slot_tables(neighbors, lax.axis_index("region"))
    keep = (neighbors[:, 4:6] >= 0).astype(F32)
    keep = jnp.pad(keep, ((0, BP - BD), (0, 0)))
    lkeep, hkeep = keep[:, 0:1], keep[:, 1:2]
    occ = jnp.pad(occupancy.astype(F32), ((0, BP - BD), (0, 0))).reshape(BP, 4, 16).swapaxes(0, 1)
    feat = features.reshape(BD * VOX, CH)
    cot = cotangent.reshape(BD * VOX, CH)
    w = weight.reshape(TAPS * CH, CH)

    dma = pltpu.SemaphoreType.DMA
    brick_rows = pltpu.VMEM((BP * VOX, CH), F32)
    pad_shape = pltpu.VMEM((6, 6, 6, BP, CH), BF)
    slot_shape = pltpu.VMEM((SLOTS, 16, CH), BF)
    plane_shape = pltpu.VMEM((4, 4, BP, CH), BF)
    half_shape = pltpu.VMEM((HALF_T, CH, CH), F32)
    tile_shape = pltpu.VMEM((HALF_T, 8, CH), F32)
    output, input_grad, total = pl.pallas_call(
        section_kernel,
        out_shape=(vmem((BD * VOX, CH), BF), vmem((BD * VOX, CH), BF), vmem((TPAD, CH, CH), F32)),
        in_specs=[IN_VMEM] * 6 + [IN_SMEM] * 2,
        out_specs=(IN_VMEM,) * 3,
        scratch_shapes=[
            pad_shape, pad_shape, pltpu.VMEM((TAPS * CH, CH), BF),
            brick_rows, brick_rows, brick_rows,
            pltpu.VMEM((4 * BP, 16, CH), F32),
            slot_shape, slot_shape, slot_shape, slot_shape,
            plane_shape, plane_shape, plane_shape, plane_shape,
            pltpu.VMEM((CH, BP * VOX), BF),
            pltpu.VMEM((TPAD, CH, CH), F32),
            half_shape, tile_shape, tile_shape,
            pltpu.VMEM((HALF_T * 8, CH), BF),
            pltpu.VMEM((NCORE, NXY, HALF_T * 8, CH), BF),
            half_shape,
            pltpu.VMEM((NXY, HALF_T, 8, CH), F32),
            pltpu.VMEM((NZ, 8, CH), F32),
            dma, dma, dma((2,)), dma((2,)), dma, dma, dma((2,)), dma((2,)),
        ] + [dma((2,))] * 6,
        compiler_params=params(collective_id=0, has_side_effects=True),
        name="section",
    )(feat, cot, w, occ, lkeep, hkeep, source, recv_slot)

    weight_grad = total[:TAPS] * (BD * REG * SLB * float(VOX)) ** -0.5
    return output.reshape(features.shape), input_grad.reshape(features.shape), weight_grad


def solution(mesh):
    return jax.shard_map(
        shards,
        mesh=mesh,
        in_specs=(
            P(("region", "slab"), None, None, None, None),
            P(),
            P(("region", "slab"), None, None, None, None),
            P(("region", "slab"), None),
            P(("region", "slab"), None),
        ),
        out_specs=(
            P(("region", "slab"), None, None, None, None),
            P(("region", "slab"), None, None, None, None),
            P(),
        ),
        check_vma=False,
    )
```

time: 661 us -> 160 us (0.24)
  waiting for transfers between devices: 518 us -> 0 us
  Pallas kernels: 0 us -> 147 us
  matrix products: 43 us -> 0 us
  starting transfers between devices: 35.7 us -> 0 us
  local copies, waits for them, and re-layouts: 29.3 us -> 6.24 us
  between operations: 15.7 us -> 0.68 us
    psum x1 -> x0, waiting for transfers between devices: 466 us -> none  [shards(): summed = lax.psum(local_grad, ('region', 'slab'))]
    pallas_call x0 -> x1, Pallas kernels: none -> 147 us  [shards(): pl.pallas_call(section_kernel, out_shape=(vmem((BD * VOX, CH), BF), vmem(...]
    all_to_all x2 -> x0, waiting for transfers between devices: 45.5 us -> none  [brick_pads(): lax.all_to_all(outgoing, 'region', split_axis=0, concat_axis=0, tiled=True)]
    dot_general x85 -> x0, matrix products: 43 us -> none  [the longest x27 27.3 us: shards(): jnp.einsum('rc,rd->cd', window, flat_grad, preferred_element_type=jnp.flo...]
    all_to_all x2 -> x0, starting transfers between devices: 28.2 us -> none  [brick_pads(): lax.all_to_all(outgoing, 'region', split_axis=0, concat_axis=0, tiled=True)]
    slice x63 -> x2, local copies, waits for them, and re-layouts: 16 us -> 0.76 us  [the longest x1 0.69 us: shards(): keep = (neighbors[:, 4:6] >= 0).astype(F32)]
    ppermute x4 -> x0, starting transfers between devices: 7.47 us -> none  [the longest x2 4.88 us: with_halo(): lax.ppermute(lax.slice_in_dim(block, 0, width, axis=dim), axis, backward)]
  transfers between devices with their start and end apart: 7 -> 0, of which waited for: 4 -> 0; matrix products, arithmetic and copies ran while one was open for 5% -> 0% of each run, Pallas kernels for 0% -> 0%
where the time goes in v2:
time: 160 us
  Pallas kernels  147 us (92%)
  local copies, waits for them, and re-layouts  6.24 us (4%)
  other arithmetic  6.11 us (4%)
    pallas_call x1, Pallas kernels, shards(): pl.pallas_call(section_kernel, out_shape=(vmem((BD * VOX, CH), BF), vmem(...  147 us
    unnamed x10, local copies, waits for them, and re-layouts  4.89 us

profile of v2, /device:TPU:25, one launch (start us, length us, event | category | flops | bytes accessed | tf_op | source)
XLA Modules:
  0.0 159.9 jit_solution(10982317321504160846)
XLA Ops:
  0.7 0.7 slice.15
  1.4 0.7 fusion.4
  2.1 0.1 ge.33
  2.1 0.1 and.74
  2.2 0.7 slice_divide_fusion
  2.9 0.1 div.39
  3.0 0.1 rem.87
  3.1 0.2 convert_reduce_fusion
  3.3 0.1 select_reduce_fusion.source_ref
  3.4 0.1 reduce_sum.32
  3.5 0.7 fusion.3
  4.2 0.1 reshape.198.recv_slot
  4.3 0.1 copy.18
  4.4 0.7 convert_element_type.14
  5.1 0.1 copy.19
  5.2 0.1 fusion.11
  5.3 0.1 copy.16
  5.4 0.0 copy-start
  5.4 1.2 copy-done
  6.6 0.0 copy-start.1
  6.6 1.0 copy-done.1
  7.6 0.0 copy-start.2
  7.6 1.0 copy-done.2
  8.6 146.9 %section.1 = (bf16[1664,128]{1,0:T(8,128)(2,1)S(1)}, bf16[1664,128]{1,0:T(8,128)(2,1)S(1)}, f32[28,128,128]{2,1,0:T(8,128)}) custom-call(bf16[1664,128]{1,0:T(8,128)(2,1)S(1)} %bitcast.11, bf16[1664,128]{1,0:T(8,128)(2,1)S(1)} %bitcast.12, bf16[3456,128]{1,0:T(8,128)(2,1)S(1)} %bitcast.8, f32[4,32,16]{2,1,0:T(8,128)S(1)} %bitcast.13, ...), custom_call_target="tpu_custom_call" | custom-call | tf_op jit(solution)/shard_map/section/pallas_call | solution.py:424
  155.5 2.9 %slice_multiply_fusion = f32[27,128,128]{2,1,0:T(8,128)} fusion(f32[28,128,128]{2,1,0:T(8,128)} %get-tuple-element.8), kind=kLoop, calls=%fused_computation | loop fusion | flops 442368 | bytes 3538944 | tf_op jit(solution)/shard_map/mul | solution.py:449
  158.4 0.8 copy.22
  159.2 0.8 copy.23
  (8 shorter events, 0.1 us)
Async XLA Ops:
  5.4 1.2 copy-start
  6.6 1.0 copy-start.1
  7.6 1.0 copy-start.2

commit v3 on v2

--- a/solution.py
+++ b/solution.py
@@ -24,7 +24,7 @@
 HALF_T = 14
 TPAD = 2 * HALF_T
 CUTS = (1, 50, 70, 80, 90, REG)
-VMEM_LIMIT = 50 * 1024 * 1024
+VMEM_LIMIT = 63 * 1024 * 1024
 
 
 def params(**kw):
@@ -37,7 +37,7 @@
 
 IN_VMEM = pl.BlockSpec(memory_space=pltpu.VMEM)
 IN_SMEM = pl.BlockSpec(memory_space=pltpu.SMEM)
-IN_ANY = pl.BlockSpec(memory_space=pl.ANY)
+IN_HBM = pl.BlockSpec(memory_space=pltpu.HBM)
 
 
 def face_voxels(side):
@@ -67,11 +67,16 @@
                     pad[c, a, b] = jnp.zeros((BP, CH), BF)
 
 
-def build_halo(pad, recv, slot_ref, low, high, lkeep, hkeep, faces):
+def build_halo(pad, recv, slot_ref, low, high, near_rows, faces):
+    kept = jnp.concatenate(
+        [(near_rows[...] >= 0).astype(F32), jnp.zeros((CH - 8, CH), F32)], axis=0).T[0:BP]
+    lkeep = jnp.broadcast_to(kept[:, 4:5], (BP, CH)) > 0
+    hkeep = jnp.broadcast_to(kept[:, 5:6], (BP, CH)) > 0
+    nothing = jnp.zeros((BP, CH), F32)
     for i in range(4):
         for j in range(4):
-            pad[i + 1, j + 1, 0] = (low[i, j].astype(F32) * lkeep[...]).astype(BF)
-            pad[i + 1, j + 1, 5] = (high[i, j].astype(F32) * hkeep[...]).astype(BF)
+            pad[i + 1, j + 1, 0] = jnp.where(lkeep, low[i, j].astype(F32), nothing).astype(BF)
+            pad[i + 1, j + 1, 5] = jnp.where(hkeep, high[i, j].astype(F32), nothing).astype(BF)
     for side in range(4):
 
         def body(b, carry):
@@ -90,17 +95,32 @@
                     pad[a + 1, 5 * (side - 2), b + 1] = slab
 
 
-def conv_plane(pad, w_ref, plane):
+def pair_taps(pairs, tap_of):
+    for n in range(9):
+        for c in range(4):
+            for e in range(2):
+                block = tap_of(3 * n + c - e) if 0 <= c - e <= 2 else jnp.zeros((CH, CH), BF)
+                pairs[512 * n + CH * c : 512 * n + CH * (c + 1), CH * e : CH * (e + 1)] = block
+
+
+def conv_plane(pad, pairs, plane):
     acc = None
     for o1 in range(3):
-        for o2 in range(3):
-            lhs = jnp.concatenate(
-                [pad[plane + o1, o2 : o2 + 4, o3 : o3 + 4].reshape(16 * BP, CH) for o3 in range(3)],
-                axis=1)
-            tap = 9 * o1 + 3 * o2
-            term = jnp.dot(lhs, w_ref[tap * CH : (tap + 3) * CH, :], preferred_element_type=F32)
-            acc = term if acc is None else acc + term
+        halves = []
+        for p in range(2):
+            halves.append(jnp.concatenate(
+                [pad[plane + o1, o2 : o2 + 4, 2 * p + c].reshape(4 * BP, CH) for o2 in range(3) for c in range(4)],
+                axis=1))
+        lhs = jnp.concatenate(halves, axis=0)
+        term = jnp.dot(lhs, pairs[1536 * o1 : 1536 * (o1 + 1), :], preferred_element_type=F32)
+        acc = term if acc is None else acc + term
     return acc
+
+
+def voxel_rows(values, t):
+    j, k = t // 4, t % 4
+    row = (k // 2) * 4 * BP + j * BP
+    return values[row : row + BP, (k % 2) * CH : (k % 2 + 1) * CH]
 
 
 def place(axis_region, slab):
@@ -143,9 +163,10 @@
     pltpu.make_async_copy(ref, ref, sem).wait()
 
 
-def section_kernel(feat, cot, w_ref, occ, lkeep, hkeep, source_ref, recv_slot,
-                   out, input_grad, total,
-                   padf, padg, wflip, rows, crows, outs, faces, slots, slots2, recv, recv2,
+def section_kernel(feat_hbm, cot_hbm, w_hbm, occupancy, near, source_ref, recv_slot,
+                   out, input_grad, total_bf,
+                   feat, cot, w_ref, occ, total, near_rows, i_sem,
+                   padf, padg, taps_f, taps_b, rows, crows, outs, faces, slots, slots2, recv, recv2,
                    low, high, low2, high2, gt, grad,
                    part, col, mine, half_bf, all_bf, got0, got1, got2,
                    s1, r1, zs1, zr1, s2, r2, zs2, zr2, a_sem, b_sem, c_sem, d_sem, e_sem, f_sem):
@@ -166,6 +187,10 @@
 
     partner = {"region": region_of(x, z, 1 - core), "slab": slab}
 
+    fetch = [pltpu.make_async_copy(a, b, i_sem.at[n])
+             for n, (a, b) in enumerate(((feat_hbm, feat), (cot_hbm, cot), (w_hbm, w_ref)))]
+    fetch[0].start()
+
     barrier = pltpu.get_barrier_semaphore()
 
     def greet(k, carry):
@@ -185,6 +210,10 @@
 
     lax.fori_loop(0, NX * (SLB - 1), greet_slabs, 0)
 
+    near_rows[...] = jnp.full((8, CH), -1, jnp.int32)
+    near_rows[0:6, 0:BD] = near[...]
+
+    fetch[0].wait()
     rows[0 : BD * VOX, :] = feat[...].astype(F32)
     rows[BD * VOX :, :] = jnp.zeros((BP * VOX - BD * VOX, CH), F32)
     for v in range(VOX):
@@ -197,10 +226,17 @@
         copy.start()
     pack_and_send(me, slab, 1, REG, faces, source_ref, slots, recv, s1, r1)
 
+    fetch[2].start()
+    fetch[1].start()
+    for p in range(4):
+        occ[p] = jnp.zeros((BP, 16), F32)
+        occ[p, 0:BD, :] = occupancy[:, 16 * p : 16 * p + 16].astype(F32)
     zero_rim(padf)
     zero_rim(padg)
-    for t in range(TAPS):
-        wflip[t * CH : (t + 1) * CH, :] = w_ref[(TAPS - 1 - t) * CH : (TAPS - t) * CH, :].T
+    fetch[2].wait()
+    pair_taps(taps_f, lambda t: w_ref[t * CH : (t + 1) * CH, :])
+    pair_taps(taps_b, lambda t: w_ref[(TAPS - 1 - t) * CH : (TAPS - t) * CH, :].T)
+    fetch[1].wait()
     crows[0 : BD * VOX, :] = cot[...].astype(F32)
     crows[BD * VOX :, :] = jnp.zeros((BP * VOX - BD * VOX, CH), F32)
     for t in range(TAPS, TPAD):
@@ -215,13 +251,13 @@
     wait_bytes(recv.at[peers], r1)
     wait_bytes(slots.at[peers], s1)
 
-    build_halo(padf, recv, recv_slot, low, high, lkeep, hkeep, faces)
+    build_halo(padf, recv, recv_slot, low, high, near_rows, faces)
 
     def plane_body(plane, carry):
-        pre = conv_plane(padf, w_ref, plane)
+        pre = conv_plane(padf, taps_f, plane)
         mask = occ[plane]
         for t in range(16):
-            u = pre[t * BP : (t + 1) * BP, :]
+            u = voxel_rows(pre, t)
             s = 1.0 / (1.0 + jnp.exp(-u))
             m = mask[:, t : t + 1]
             f = padf[plane + 1, t // 4 + 1, t % 4 + 1].astype(F32)
@@ -258,6 +294,12 @@
         return carry
 
     lax.fori_loop(0, 9, tap_body, 0)
+
+    def back_plane(plane):
+        back = conv_plane(padg, taps_b, plane)
+        for t in range(16):
+            c = crows[pl.ds(16 * plane + t, BP, stride=VOX), :]
+            outs[pl.ds(16 * plane + t, BP, stride=VOX), :] = c + voxel_rows(back, t)
 
     own = pl.ds(core * HALF_T, HALF_T)
     other_half = pl.ds((1 - core) * HALF_T, HALF_T)
@@ -353,6 +395,15 @@
     lax.fori_loop(1, NXY, send4, 0)
     send_faces(4)
     all_bf[core, q] = half_bf[...]
+
+    for copy in pair:
+        copy.wait()
+    wait_bytes(recv2.at[peers], r2)
+    build_halo(padg, recv2, recv_slot, low2, high2, near_rows, faces)
+    back_plane(0)
+    back_plane(1)
+    back_plane(2)
+    back_plane(3)
     span4 = all_bf.at[0, pl.ds(0, NXY - 1)]
     wait_bytes(span4, e_sem.at[1])
     wait_bytes(span4, e_sem.at[0])
@@ -360,28 +411,14 @@
     pair1 = pltpu.make_async_remote_copy(
         all_bf.at[core], all_bf.at[core], f_sem.at[0], f_sem.at[1], device_id=partner, device_id_type=MESH)
     pair1.start()
+    input_grad[...] = outs[0 : BD * VOX, :].astype(BF)
+    wait_bytes(slots2.at[peers], s2)
     pair1.wait()
     for c in range(NCORE):
         for k in range(NXY):
             total[HALF_T * c : HALF_T * (c + 1), 8 * k : 8 * k + 8, :] = (
                 all_bf[c, k].astype(F32).reshape(HALF_T, 8, CH))
-
-    for copy in pair:
-        copy.wait()
-    wait_bytes(recv2.at[peers], r2)
-    wait_bytes(slots2.at[peers], s2)
-    build_halo(padg, recv2, recv_slot, low2, high2, lkeep, hkeep, faces)
-
-    def back_body(plane, carry):
-        back = conv_plane(padg, wflip, plane)
-        for t in range(16):
-            c = crows[pl.ds(16 * plane + t, BP, stride=VOX), :]
-            outs[pl.ds(16 * plane + t, BP, stride=VOX), :] = c + back[t * BP : (t + 1) * BP, :]
-        return carry
-
-    lax.fori_loop(0, 4, back_body, 0)
-    input_grad[...] = outs[0 : BD * VOX, :].astype(BF)
-
+    total_bf[...] = total[0:TAPS].astype(BF)
 
 def slot_tables(neighbors, me):
     linked = neighbors.T[:4].reshape(4 * BD)
@@ -406,10 +443,6 @@
 
 def shards(features, weight, cotangent, occupancy, neighbors):
     source, recv_slot = slot_tables(neighbors, lax.axis_index("region"))
-    keep = (neighbors[:, 4:6] >= 0).astype(F32)
-    keep = jnp.pad(keep, ((0, BP - BD), (0, 0)))
-    lkeep, hkeep = keep[:, 0:1], keep[:, 1:2]
-    occ = jnp.pad(occupancy.astype(F32), ((0, BP - BD), (0, 0))).reshape(BP, 4, 16).swapaxes(0, 1)
     feat = features.reshape(BD * VOX, CH)
     cot = cotangent.reshape(BD * VOX, CH)
     w = weight.reshape(TAPS * CH, CH)
@@ -423,11 +456,14 @@
     tile_shape = pltpu.VMEM((HALF_T, 8, CH), F32)
     output, input_grad, total = pl.pallas_call(
         section_kernel,
-        out_shape=(vmem((BD * VOX, CH), BF), vmem((BD * VOX, CH), BF), vmem((TPAD, CH, CH), F32)),
-        in_specs=[IN_VMEM] * 6 + [IN_SMEM] * 2,
+        out_shape=(vmem((BD * VOX, CH), BF), vmem((BD * VOX, CH), BF), vmem((TAPS, CH, CH), BF)),
+        in_specs=[IN_HBM] * 3 + [IN_VMEM] * 2 + [IN_SMEM] * 2,
         out_specs=(IN_VMEM,) * 3,
         scratch_shapes=[
-            pad_shape, pad_shape, pltpu.VMEM((TAPS * CH, CH), BF),
+            pltpu.VMEM((BD * VOX, CH), BF), pltpu.VMEM((BD * VOX, CH), BF), pltpu.VMEM((TAPS * CH, CH), BF),
+            pltpu.VMEM((4, BP, 16), F32), pltpu.VMEM((TPAD, CH, CH), F32),
+            pltpu.VMEM((8, CH), jnp.int32), dma((3,)),
+            pad_shape, pad_shape, pltpu.VMEM((9 * 512, 256), BF), pltpu.VMEM((9 * 512, 256), BF),
             brick_rows, brick_rows, brick_rows,
             pltpu.VMEM((4 * BP, 16, CH), F32),
             slot_shape, slot_shape, slot_shape, slot_shape,
@@ -444,9 +480,9 @@
         ] + [dma((2,))] * 6,
         compiler_params=params(collective_id=0, has_side_effects=True),
         name="section",
-    )(feat, cot, w, occ, lkeep, hkeep, source, recv_slot)
-
-    weight_grad = total[:TAPS] * (BD * REG * SLB * float(VOX)) ** -0.5
+    )(feat, cot, w, occupancy, neighbors.T, source, recv_slot)
+
+    weight_grad = total.astype(F32) * (BD * REG * SLB * float(VOX)) ** -0.5
     return output.reshape(features.shape), input_grad.reshape(features.shape), weight_grad
 
 

time: 160 us -> 156 us (0.975)
  local copies, waits for them, and re-layouts: 6.24 us -> 2.53 us
    unnamed x10 -> x6, local copies, waits for them, and re-layouts: 4.89 us -> 1.52 us
where the time goes in v3:
time: 156 us; the launch traced here: 155 us
  Pallas kernels  147 us (94%)
  other arithmetic  5.67 us (4%)
  local copies, waits for them, and re-layouts  2.53 us (2%)
    pallas_call x1, Pallas kernels, shards(): pl.pallas_call(section_kernel, out_shape=(vmem((BD * VOX, CH), BF), vmem(...  147 us

profile of v3, /device:TPU:25, one launch (start us, length us, event | category | flops | bytes accessed | tf_op | source)
XLA Modules:
  0.0 155.4 jit_solution(15539426897672080368)
XLA Ops:
  0.7 0.7 fusion.4
  1.4 0.1 ge.25
  1.5 0.1 and.74
  1.5 0.7 slice_divide_fusion
  2.2 0.1 div.39
  2.3 0.1 rem.87
  2.4 0.2 convert_reduce_fusion
  2.6 0.7 select_reduce_fusion.source_ref
  3.3 0.1 reduce_sum.32
  3.4 0.7 fusion.3
  4.1 0.6 reshape.194.recv_slot
  4.7 146.5 %section.1 = (bf16[1664,128]{1,0:T(8,128)(2,1)}, bf16[1664,128]{1,0:T(8,128)(2,1)}, bf16[27,128,128]{2,1,0:T(8,128)(2,1)}) custom-call(bf16[1664,128]{1,0:T(8,128)(2,1)} %bitcast.7, bf16[1664,128]{1,0:T(8,128)(2,1)} %bitcast.8, bf16[3456,128]{1,0:T(8,128)(2,1)} %bitcast.6, s32[26,64]{1,0:T(8,128)} %occupancy.1, s32[6,26]{1,0:T(8,128)} %bitcast.14, ...), custom_call_target="tpu_custom_call" | custom-call | tf_op jit(solution)/shard_map/section/pallas_call | solution.py:457
  151.2 0.0 copy-start.1
  151.2 0.0 copy-start
  151.2 2.7 %convert_multiply_fusion = f32[27,128,128]{2,1,0:T(8,128)} fusion(bf16[27,128,128]{2,1,0:T(8,128)(2,1)} %get-tuple-element.8), kind=kLoop, calls=%fused_computation | loop fusion | flops 884736 | bytes 2654208 | tf_op jit(solution)/shard_map/mul | solution.py:485
  153.9 0.0 copy-done.1
  153.9 0.8 copy.10
  154.6 0.0 copy-done
  154.6 0.8 copy.11
  (5 shorter events, 0.1 us)
Async XLA Ops:
  151.2 2.7 %copy-start.1 = (bf16[1664,128]{1,0:T(8,128)(2,1)S(1)}, bf16[1664,128]{1,0:T(8,128)(2,1)}, u32[]{:S(2)}) copy-start(bf16[1664,128]{1,0:T(8,128)(2,1)} %get-tuple-element.6) | copy-start | bytes 1277956
  151.2 3.4 %copy-start = (bf16[1664,128]{1,0:T(8,128)(2,1)S(1)}, bf16[1664,128]{1,0:T(8,128)(2,1)}, u32[]{:S(2)}) copy-start(bf16[1664,128]{1,0:T(8,128)(2,1)} %get-tuple-element.7) | copy-start | bytes 1277956

commit v4 on v3

--- a/solution.py
+++ b/solution.py
@@ -80,10 +80,10 @@
     for side in range(4):
 
         def body(b, carry):
-            faces[side * BP + b] = recv[slot_ref[side * BP + b]].astype(F32)
+            faces[side * BP + b] = recv[slot_ref[side * BD + b]].astype(F32)
             return carry
 
-        lax.fori_loop(0, BP, body, 0)
+        lax.fori_loop(0, BD, body, 0)
     faces = faces.reshape(4, BP * 16, CH)
     for side in range(4):
         for a in range(4):
@@ -283,6 +283,7 @@
                 padg[i + 1, j + 1, 1:5].reshape(4 * BP, CH).T)
 
     def tap_body(n, carry):
+        n = lax.rem(n + 4 * (1 - core), 9)
         o1 = n // 3
         o2 = lax.rem(n, 3)
         rhs = jnp.concatenate(
@@ -293,7 +294,7 @@
             grad[3 * n + o3] = res[:, CH * o3 : CH * (o3 + 1)].T
         return carry
 
-    lax.fori_loop(0, 9, tap_body, 0)
+    lax.fori_loop(0, 5, tap_body, 0)
 
     def back_plane(plane):
         back = conv_plane(padg, taps_b, plane)
@@ -306,6 +307,7 @@
     pair0 = pltpu.make_async_remote_copy(
         grad.at[other_half], got0, a_sem.at[0], a_sem.at[1], device_id=partner, device_id_type=MESH)
     pair0.start()
+    lax.fori_loop(5, 9, tap_body, 0)
     out[...] = outs[0 : BD * VOX, :].astype(BF)
     pair0.wait()
 
@@ -433,8 +435,6 @@
     recv_rank = jnp.sum(same & (wanted[None, :] < wanted[:, None]), axis=1, dtype=jnp.int32)
     send_slot = jnp.where(present, owner * 2 + send_rank, -1)
     recv_slot = jnp.where(present, owner * 2 + recv_rank, 2 * me)
-    recv_slot = jnp.pad(recv_slot.reshape(4, BD), ((0, 0), (0, BP - BD)), constant_values=0)
-    recv_slot = jnp.where(jnp.arange(BP)[None, :] < BD, recv_slot, 2 * me).reshape(4 * BP)
     slot = jnp.arange(SLOTS, dtype=jnp.int32)
     face = side * BP + key - side * BD
     source = jnp.sum(jnp.where(send_slot[None, :] == slot[:, None], face[None, :], 0), axis=1, dtype=jnp.int32)

time: 156 us -> 152 us (0.974)
  Pallas kernels: 147 us -> 144 us
    pallas_call x1, Pallas kernels: 147 us -> 144 us  [shards(): pl.pallas_call(section_kernel, out_shape=(vmem((BD * VOX, CH), BF), vmem(...]
where the time goes in v4:
time: 152 us
  Pallas kernels  144 us (95%)
  other arithmetic  5.47 us (4%)
  local copies, waits for them, and re-layouts  1.86 us (1%)
    pallas_call x1, Pallas kernels, shards(): pl.pallas_call(section_kernel, out_shape=(vmem((BD * VOX, CH), BF), vmem(...  144 us

profile of v4, /device:TPU:25, one launch (start us, length us, event | category | flops | bytes accessed | tf_op | source)
XLA Modules:
  0.0 151.8 jit_solution(16956924155193261565)
XLA Ops:
  0.7 0.7 fusion
  1.4 0.1 and.73
  1.4 0.1 ge.24
  1.5 0.7 slice_divide_fusion
  2.2 0.1 div.38
  2.3 0.1 rem.86
  2.4 0.2 convert_reduce_fusion
  2.6 0.5 add_select_fusion.1
  3.1 0.7 select_reduce_fusion.source_ref
  3.8 143.8 %section.1 = (bf16[1664,128]{1,0:T(8,128)(2,1)}, bf16[1664,128]{1,0:T(8,128)(2,1)}, bf16[27,128,128]{2,1,0:T(8,128)(2,1)}) custom-call(bf16[1664,128]{1,0:T(8,128)(2,1)} %bitcast.7, bf16[1664,128]{1,0:T(8,128)(2,1)} %bitcast.8, bf16[3456,128]{1,0:T(8,128)(2,1)} %bitcast.6, s32[26,64]{1,0:T(8,128)} %occupancy.1, s32[6,26]{1,0:T(8,128)} %bitcast.13, ...), custom_call_target="tpu_custom_call" | custom-call | tf_op jit(solution)/shard_map/section/pallas_call | solution.py:457
  147.6 0.0 copy-start.1
  147.6 0.0 copy-start
  147.6 2.7 %convert_multiply_fusion = f32[27,128,128]{2,1,0:T(8,128)} fusion(bf16[27,128,128]{2,1,0:T(8,128)(2,1)} %get-tuple-element.8), kind=kLoop, calls=%fused_computation | loop fusion | flops 884736 | bytes 2654208 | tf_op jit(solution)/shard_map/mul | solution.py:485
  150.3 0.0 copy-done.1
  150.3 0.8 copy.10
  151.0 0.0 copy-done
  151.1 0.8 copy.11
  (2 shorter events, 0.0 us)
Async XLA Ops:
  147.6 2.7 %copy-start.1 = (bf16[1664,128]{1,0:T(8,128)(2,1)S(1)}, bf16[1664,128]{1,0:T(8,128)(2,1)}, u32[]{:S(2)}) copy-start(bf16[1664,128]{1,0:T(8,128)(2,1)} %get-tuple-element.6) | copy-start | bytes 1277956
  147.6 3.4 %copy-start = (bf16[1664,128]{1,0:T(8,128)(2,1)S(1)}, bf16[1664,128]{1,0:T(8,128)(2,1)}, u32[]{:S(2)}) copy-start(bf16[1664,128]{1,0:T(8,128)(2,1)} %get-tuple-element.7) | copy-start | bytes 1277956
